TPU v7x, 512 devices: a whole 4x8x8 slice. The times are simulated.
512 devices in a mesh: node: 64 (over z, y_hi, x), local: 8 (over y_lo, core).
Axes of the slice: x: 4, y: 8 (y_hi: 2, y_lo: 4; y = y_hi * 4 + y_lo), z: 8, core: 2. Of those that a mesh axis runs over, the one named last changes fastest.
Arguments:
- normed_input: bfloat16 [131072, 4096], P(('node', 'local')), may hold values from -60 to 60
- key_weight: bfloat16 [4096, 512], P(('node', 'local')), may hold values from -0.09375 to 0.09375
- key_cotangent: bfloat16 [131072, 512], P(('node', 'local')), may hold values from -60 to 60
Outputs:
- keys: bfloat16 [131072, 512], P(('node', 'local'))
- input_grad: bfloat16 [131072, 4096], P(('node', 'local'))
- weight_update: float32 [4096, 512], P(('node', 'local'))
All inputs are finite; a program needn't handle non-finite values.
Results may differ from a plain program's by a relative error of at most 0.0029.
Values may be sent and summed in bfloat16 or wider, within the bound.
A program may use at most 64 MiB of HBM per device.

v0:
```python
import jax
import jax.numpy as jnp
from jax import lax
from jax.sharding import PartitionSpec as P


def body(normed_input, key_weight, key_cotangent):
    tokens_here, width = normed_input.shape
    rows, kv_width = key_weight.shape
    node_count = lax.axis_size("node")
    local_count = lax.axis_size("local")
    local_place = lax.axis_index("local")
    full_weight = lax.all_gather(key_weight, ("node", "local"), axis=0, tiled=True)
    keys = jnp.dot(normed_input, full_weight, preferred_element_type=jnp.float32).astype(
        jnp.bfloat16
    )
    weight_blocks = full_weight.reshape(node_count, local_count, rows, kv_width)
    secondary = lax.dynamic_index_in_dim(weight_blocks, local_place, 1, keepdims=False)
    grad_blocks = jnp.einsum(
        "tc,nkc->tnk",
        key_cotangent,
        lax.all_gather(secondary, "local", axis=1, tiled=True),
        preferred_element_type=jnp.float32,
    ).astype(jnp.bfloat16)
    input_grad = grad_blocks.reshape(tokens_here, width)
    term = jnp.einsum(
        "td,tc->dc", normed_input, key_cotangent, preferred_element_type=jnp.float32
    ).astype(jnp.bfloat16)
    term_blocks = term.reshape(node_count, local_count, rows, kv_width)
    received = lax.all_to_all(term_blocks, "local", split_axis=1, concat_axis=1, tiled=True)
    partial_sum = jnp.sum(received, axis=1, dtype=jnp.float32)
    weight_grad = lax.psum_scatter(partial_sum, "node", scatter_dimension=0, tiled=True)
    weight_grad = weight_grad.reshape(rows, kv_width)
    square_sum = lax.psum(jnp.sum(weight_grad * weight_grad), ("node", "local"))
    weight_update = weight_grad * lax.rsqrt(square_sum / (width * kv_width) + 1e-06)
    return (keys, input_grad, weight_update)


def solution(mesh):
    placed = (P(("node", "local"), None), P(("node", "local"), None), P(("node", "local"), None))
    return jax.shard_map(
        body,
        mesh=mesh,
        in_specs=placed,
        out_specs=(
            P(("node", "local"), None),
            P(("node", "local"), None),
            P(("node", "local"), None),
        ),
        check_vma=False,
    )
```

profile of v0, /device:TPU:1, one launch (start us, length us, event | category | flops | bytes accessed | tf_op | source)
XLA Modules:
  0.0 952.7 jit_solution(18416115704988318343)
XLA Ops:
  8.0 0.0 copy-start
  8.0 0.0 all-gather.4.cloned.1.call-start
  8.1 0.7 all-gather.4.cloned.1.call-update
  8.7 0.0 reduce-scatter.2.cloned.1.call-start
  8.8 0.8 copy-done
  9.6 2.2 convolution_convert_fusion
  11.8 0.4 copy.10
  12.2 104.8 %all_to_all.5 = bf16[64,8,8,512]{3,2,0,1:T(8,128)(2,1)S(1)} all-to-all(bf16[64,8,8,512]{3,2,0,1:T(8,128)(2,1)S(1)} %copy.10), channel_id=1, replica_groups=mesh['node'=64,'local'=8] {'local'}, dimensions={1} | all-to-all | bytes 8388608 | tf_op jit(solution)/shard_map/all_to_all | solution.py:30
  117.0 1.6 convert_reduce_fusion
  118.6 0.0 reduce-scatter.2.cloned.1.call-update
  118.6 0.0 all-gather.6.cloned.1.call-start
  118.7 702.9 %all-gather.4.cloned.1.call-done = bf16[4096,512]{1,0:T(8,128)(2,1)} async-done(((bf16[8,512]{1,0:T(8,128)(2,1)}), bf16[4096,512]{1,0:T(8,128)(2,1)}) %all-gather.4.cloned.1.call-update) | async-done | bytes 4194320 | tf_op jit(solution)/shard_map/all_gather | solution.py:13
  821.6 1.9 dynamic-slice_bitcast_fusion
  823.5 0.0 copy-start.1
  823.5 0.0 all-gather.6.cloned.1.call-update
  823.5 0.0 reduce-scatter.2.cloned.1.call-done
  823.5 0.0 copy-start.2
  823.5 1.4 multiply_reduce_fusion
  824.9 4.1 convolution_convert_fusion.1
  829.1 106.1 %psum.7 = f32[]{:T(128)} all-reduce(f32[]{:T(128)} %multiply_reduce_fusion), channel_id=1, replica_groups=mesh['node'=64,'local'=8] {'node','local'}, use_global_device_ids=true, to_apply=%region_3.4 | all-reduce | flops 1 | bytes 8 | tf_op jit(solution)/shard_map/psum | solution.py:34
  935.8 0.0 copy-done.2
  935.8 0.6 multiply_bitcast_fusion
  936.4 0.0 all-gather.6.cloned.1.call-done
  936.4 0.0 copy-done.1
  936.4 4.8 fusion.2
  941.2 4.1 copy.11
Async XLA Ops:
  8.0 1.6 copy-start
  8.0 813.5 %all-gather.4.cloned.1.call-start = ((), (), s32[]{:S(2)}) async-start(), calls=%async_computation.2 | async-start | bytes 4202496 | tf_op jit(solution)/shard_map/all_gather | solution.py:13
  8.7 814.8 %reduce-scatter.2.cloned.1.call-start = ((), (), s32[]{:S(2)}) async-start(), calls=%async_computation.3 | async-start | bytes 1064960 | tf_op jit(solution)/shard_map/reduce_scatter | solution.py:32
  118.6 817.8 %all-gather.6.cloned.1.call-start = ((), (), s32[]{:S(2)}) async-start(), calls=%async_computation.4 | async-start | bytes 4718592 | tf_op jit(solution)/shard_map/all_gather | solution.py:22
  823.5 113.0 %copy-start.1 = (bf16[256,512]{1,0:T(8,128)(2,1)S(1)}, bf16[256,512]{1,0:T(8,128)(2,1)}, u32[]{:S(2)}) copy-start(bf16[256,512]{1,0:T(8,128)(2,1)} %param.5) | copy-start | bytes 786436
  823.5 112.3 %copy-start.2 = (f32[1,8,512]{2,1,0:T(8,128)S(1)}, f32[1,8,512]{2,1,0:T(8,128)}, u32[]{:S(2)}) copy-start(f32[1,8,512]{2,1,0:T(8,128)} %reduce-scatter.2.cloned.1.call-done) | copy-start | bytes 49156
Sparse Core Ops, SparseCore 0:
  11.1 810.4 all-gather.3
  823.6 62.0 all-gather.5
Sparse Core Ops, SparseCore 1:
  118.7 390.7 reduce-scatter.1
where the time goes:
time: 953 us
  waiting for transfers between devices  704 us (74%)
  blocking collectives  211 us (22%)
  between operations  16.2 us (2%)
  matrix products  11.2 us (1%)
    all_gather x1, waiting for transfers between devices, body(): lax.all_gather(key_weight, ('node', 'local'), axis=0, tiled=True)  703 us
    psum x1, blocking collectives, body(): square_sum = lax.psum(jnp.sum(weight_grad * weight_grad), ('node', 'local'))  106 us
    all_to_all x1, blocking collectives, body(): lax.all_to_all(term_blocks, 'local', split_axis=1, concat_axis=1, tiled=T...  105 us
  transfers between devices with their start and end apart: 3, of which 1 were waited for; matrix products, arithmetic and copies ran while one was open for 1% of the time, Pallas kernels for 0%

commit v1 on v0

v1 whole, which is shorter than its diff:
```python
import jax
import jax.numpy as jnp
from jax import lax
from jax.experimental import pallas as pl
from jax.experimental.pallas import tpu as pltpu
from jax.sharding import PartitionSpec as P

MESH = pl.DeviceIdType.MESH
NX, NY, NZ = 4, 8, 8
F32, BF16 = jnp.float32, jnp.bfloat16
ORDER = (4, 3, 5, 2, 6, 1, 7, 0)


def mod(a, n):
    return lax.rem(a + n, n)


def dev(x, y, z, c):
    return ((z * 2 + lax.div(y, 4)) * 4 + x, lax.rem(y, 4) * 2 + c)


def copy_to(src, dst, send_sem, recv_sem, device):
    return pltpu.make_async_remote_copy(
        src_ref=src,
        dst_ref=dst,
        send_sem=send_sem,
        recv_sem=recv_sem,
        device_id=device,
        device_id_type=MESH,
    )


def kernel(
    x_ref, w_ref, c_ref, keys_ref, grad_ref, update_ref,
    weight, shard, shard_in, away, pair_in, term, ring_in, block, block_in,
    slab, slab_in, mine, mine_in, squares, squares_in, keys_sum,
    shard_s, shard_r, pair_s, pair_r, gz_s, gz_r, gy_s, gy_r, gx_s, gx_r, gf_s, gf_r, gc_s, gc_r,
    ring_s, ring_r, block_s, block_r, slab_s, slab_r, mine_s, mine_r, sq_s, sq_r,
):
    node, local = lax.axis_index("node"), lax.axis_index("local")
    x = lax.rem(node, 4)
    y = lax.rem(lax.div(node, 4), 2) * 4 + lax.div(local, 2)
    z = lax.div(node, 8)
    c = lax.rem(local, 2)
    sib = 1 - c
    sibling = dev(x, y, z, sib)
    along_x = lambda k: dev(mod(x + k, NX), y, z, c)
    along_y = lambda k: dev(x, mod(y + k, NY), z, c)
    along_z = lambda k: dev(x, y, mod(z + k, NZ), c)
    place = (z, y)
    along = (along_z, along_y)
    across = (along_y, along_z)
    across_place = (y, z)
    sent = []

    def start(copy):
        copy.start()
        sent.append(copy)

    barrier = pltpu.get_barrier_semaphore()
    greeted = [along_z(k) for k in range(1, NZ)] + [along_y(k) for k in range(1, NY)]
    greeted += [dev(mod(x + k, NX), y, z, c) for k in range(1, NX)]
    greeted += [dev(mod(x + k, NX), y, z, sib) for k in range(NX)]
    for device in greeted:
        pl.semaphore_signal(barrier, inc=1, device_id=device, device_id_type=MESH)

    def terms_of(half, ref):
        cot = c_ref[:, pl.ds(pl.multiple_of(half * 256, 256), 256)]

        def one(zb, carry):
            rows = x_ref[:, pl.ds(pl.multiple_of(zb * 512, 512), 512)]
            t = lax.dot_general(
                rows, cot, (((0,), (0,)), ((), ())), preferred_element_type=F32
            ).astype(BF16)
            ref[0, zb] = t[:, :128].reshape(2, 4, 64, 128)
            tb = t[:, 128:].reshape(2, 4, 4, 16, 128)
            for yh in range(2):
                for yl in range(4):
                    ref[1, yh * 4 + yl, lax.div(zb, 4), lax.rem(zb, 4)] = tb[yh, :, yl].reshape(64, 128)
            return carry

        lax.fori_loop(0, 8, one, 0)

    w = w_ref[...].astype(F32)
    shard[0] = w[:, :256]
    shard[1] = w[:, 256:]
    terms_of(sib, away)
    pl.semaphore_wait(barrier, len(greeted))

    start(copy_to(shard.at[sib], shard_in, shard_s, shard_r, sibling))
    pairs = {}
    for o in ORDER:
        for q in range(2):
            b = mod(place[q] + o, 8)
            pairs[q, o] = copy_to(away.at[q, b], pair_in.at[q, b], pair_s.at[q, o], pair_r.at[q, o], sibling)
            start(pairs[q, o])
    terms_of(c, term)

    yh, yl = lax.div(y, 4), lax.rem(y, 4)
    copy_to(shard.at[sib], shard_in, shard_s, shard_r, sibling).wait_recv()
    own, other = shard[c], shard_in[...]
    first = jnp.where(c == 0, own, other)
    second = jnp.where(c == 0, other, own)
    weight[c, z, yh, x, yl] = jnp.concatenate([first, second], axis=0).astype(BF16)
    for k in range(1, NZ):
        spot = weight.at[c, z, yh, x, yl]
        start(copy_to(spot, spot, gz_s.at[k - 1], gz_r.at[k - 1], along_z(k)))

    def length(sign, u):
        return 4 if (sign == 0) == (u == 0) else 3

    waited = set()

    def paired(q, o, u):
        if (q, o % 8) not in waited:
            waited.add((q, o % 8))
            pairs[q, o % 8].wait_recv()
        b = mod(place[q] + o, 8)
        return b, term[q, b, u].astype(F32) + pair_in[q, b, u].astype(F32)

    def ring_copy(q, sign, u, s, b):
        return copy_to(
            term.at[q, b, u],
            ring_in.at[q, sign, u, s - 1],
            ring_s.at[q, sign, u, s - 1],
            ring_r.at[q, sign, u, s - 1],
            along[q](1 - 2 * sign),
        )

    def ring_step(s):
        for u in range(2):
            for q in range(2):
                for sign in range(2):
                    n = length(sign, u)
                    if s > n:
                        continue
                    o = (1 - 2 * sign) * (n - s + 1)
                    b, total = paired(q, o, u)
                    if s > 1:
                        ring_copy(q, sign, u, s - 1, b).wait_recv()
                        total = total + ring_in[q, sign, u, s - 2].astype(F32)
                    term[q, b, u] = total.astype(BF16)
                    start(ring_copy(q, sign, u, s, b))

    def column(h, xo, yo, lo=0, n=8):
        yy = mod(y + yo, 8)
        return weight.at[h, pl.ds(lo, n), lax.div(yy, 4), mod(x + xo, NX), lax.rem(yy, 4)]

    columns = (0, -1, 1, -2, 2, -3, 3, 4)

    def send_x(j):
        col = column(c, 0, columns[j])
        for sign in range(2):
            start(copy_to(col, col, gx_s.at[sign, j], gx_r.at[sign, j], along_x(1 - 2 * sign)))

    def gather_y(s):
        for sign in range(2):
            lo, n = (0, 8) if s < 4 else (4 * sign, 4)
            col = column(c, 0, -(1 - 2 * sign) * (s - 1), lo, n)
            start(copy_to(col, col, gy_s.at[sign, s - 1], gy_r.at[sign, s - 1], along_y(1 - 2 * sign)))

    def gathered_y(s):
        for sign in range(2):
            lo, n = (0, 8) if s < 4 else (4 * sign, 4)
            col = column(c, 0, -(1 - 2 * sign) * s, lo, n)
            copy_to(col, col, gy_s.at[sign, s - 1], gy_r.at[sign, s - 1], along_y(1 - 2 * sign)).wait_recv()

    ring_step(1)
    for k in range(1, NZ):
        spot = weight.at[c, mod(z - k, NZ), yh, x, yl]
        copy_to(spot, spot, gz_s.at[k - 1], gz_r.at[k - 1], along_z(k)).wait_recv()
    gather_y(1)
    send_x(0)
    ring_step(2)
    gathered_y(1)
    gather_y(2)
    send_x(1)
    send_x(2)
    ring_step(3)
    gathered_y(2)
    gather_y(3)
    send_x(3)
    send_x(4)
    ring_step(4)
    gathered_y(3)
    gather_y(4)
    send_x(5)
    send_x(6)

    for q in range(2):
        for u in range(2):
            b, total = paired(q, 0, u)
            for sign in range(2):
                n = length(sign, u)
                ring_copy(q, sign, u, n, b).wait_recv()
                total = total + ring_in[q, sign, u, n - 1].astype(F32)
            for j in range(4):
                if q == 0:
                    block[q, u * 4 + j] = total.reshape(4, 4, 16, 128)[:, j]
                else:
                    block[q, u * 4 + j] = total[j].reshape(4, 16, 128)
    def block_copy(q, k):
        return copy_to(
            block.at[q, mod(across_place[q] + k, 8)], block_in.at[q, k - 1],
            block_s.at[q, k - 1], block_r.at[q, k - 1], across[q](k),
        )

    for k in (4, 3, 5, 2, 6, 1, 7):
        for q in range(2):
            start(block_copy(q, k))

    gathered_y(4)
    send_x(7)

    def to_sibling(i, xo):
        part = weight.at[c, :, :, mod(x + xo, NX)]
        start(copy_to(part, part, gc_s.at[i], gc_r.at[i], sibling))

    to_sibling(0, 0)
    for j in range(8):
        for sign in range(2):
            col = column(c, -(1 - 2 * sign), columns[j])
            copy_to(col, col, gx_s.at[sign, j], gx_r.at[sign, j], along_x(1 - 2 * sign)).wait_recv()
            half = column(c, -(1 - 2 * sign), columns[j], 4 * sign, 4)
            start(copy_to(half, half, gf_s.at[sign, j], gf_r.at[sign, j], along_x(1 - 2 * sign)))
    to_sibling(1, -1)
    to_sibling(2, 1)

    for q in range(2):
        total = block[q, across_place[q]]
        for k in range(1, 8):
            block_copy(q, k).wait_recv()
            total = total + block_in[q, k - 1]
        slab[:, q] = total

    def slab_copy(k):
        return copy_to(slab.at[mod(x + k, NX)], slab_in.at[k - 1], slab_s.at[k - 1], slab_r.at[k - 1], along_x(k))

    for k in range(1, NX):
        start(slab_copy(k))

    for j in range(8):
        for sign in range(2):
            half = column(c, 2, columns[j], 4 * sign, 4)
            copy_to(half, half, gf_s.at[sign, j], gf_r.at[sign, j], along_x(1 - 2 * sign)).wait_recv()
    to_sibling(3, 2)

    total = slab[x]
    for k in range(1, NX):
        slab_copy(k).wait_recv()
        total = total + slab_in[k - 1]
    mine[0] = total[:, :8]
    mine[1] = total[:, 8:]
    start(copy_to(mine.at[sib], mine_in, mine_s, mine_r, sibling))

    sq = total * total
    sq = sq[0, :8] + sq[0, 8:] + sq[1, :8] + sq[1, 8:]

    def multiply(lo, hi):
        def one(zb, carry):
            at = pl.ds(pl.multiple_of(zb * 512, 512), 512)
            rows = x_ref[:, at]
            w0 = weight[0, zb].reshape(512, 256)
            w1 = weight[1, zb].reshape(512, 256)
            k0 = jnp.dot(rows, w0, preferred_element_type=F32)
            k1 = jnp.dot(rows, w1, preferred_element_type=F32)

            @pl.when(zb == 0)
            def _():
                keys_sum[:, :256] = k0
                keys_sum[:, 256:] = k1

            @pl.when(zb > 0)
            def _():
                keys_sum[:, :256] += k0
                keys_sum[:, 256:] += k1

            nt = (((1,), (1,)), ((), ()))
            g = lax.dot_general(c_ref[:, :256], w0, nt, preferred_element_type=F32)
            g += lax.dot_general(c_ref[:, 256:], w1, nt, preferred_element_type=F32)
            grad_ref[:, at] = g.astype(BF16)
            return carry

        lax.fori_loop(lo, hi, one, 0)

    groups = (
        [dev(mod(x + k, NX), y, z, mod(c + j, 2)) for k in range(NX) for j in range(2) if k or j],
        [along_y(k) for k in range(1, NY)],
        [along_z(k) for k in range(1, NZ)],
    )

    def square_copy(i, k):
        return copy_to(squares.at[i], squares_in.at[i, k], sq_s.at[i, k], sq_r.at[i, k], groups[i][k])

    parts = ((0, 3), (3, 6), (6, 8))
    for i in range(3):
        squares[i] = sq
        for k in range(7):
            start(square_copy(i, k))
        if i == 0:
            for n, xo in enumerate((0, -1, 1, 2)):
                part = weight.at[sib, :, :, mod(x + xo, NX)]
                copy_to(part, part, gc_s.at[n], gc_r.at[n], sibling).wait_recv()
        multiply(*parts[i])
        if i == 2:
            keys_ref[...] = keys_sum[...].astype(BF16)
        for k in range(7):
            square_copy(i, k).wait_recv()
            sq = sq + squares_in[i, k]

    scale = lax.rsqrt(jnp.full((8, 128), jnp.sum(sq) / 2097152.0 + 1e-06, F32))
    copy_to(mine.at[sib], mine_in, mine_s, mine_r, sibling).wait_recv()
    got = mine[c]
    came = mine_in[...]
    for q in range(2):
        update_ref[:, q * 128 : q * 128 + 128] = jnp.where(c == 0, got[q], came[q]) * scale
        update_ref[:, 256 + q * 128 : 384 + q * 128] = jnp.where(c == 0, came[q], got[q]) * scale
    for copy in sent:
        copy.wait_send()


def body(normed_input, key_weight, key_cotangent):
    vmem = pl.BlockSpec(memory_space=pltpu.VMEM)
    dma = pltpu.SemaphoreType.DMA
    return pl.pallas_call(
        kernel,
        out_shape=(
            jax.ShapeDtypeStruct((256, 512), BF16),
            jax.ShapeDtypeStruct((256, 4096), BF16),
            jax.ShapeDtypeStruct((8, 512), F32),
        ),
        in_specs=[vmem] * 3,
        out_specs=(vmem,) * 3,
        scratch_shapes=[
            pltpu.VMEM((2, NZ, 2, NX, 4, 16, 256), BF16),
            pltpu.VMEM((2, 8, 256), F32),
            pltpu.VMEM((8, 256), F32),
            pltpu.VMEM((2, 8, 2, 4, 64, 128), BF16),
            pltpu.VMEM((2, 8, 2, 4, 64, 128), BF16),
            pltpu.VMEM((2, 8, 2, 4, 64, 128), BF16),
            pltpu.VMEM((2, 2, 2, 4, 4, 64, 128), BF16),
            pltpu.VMEM((2, 8, 4, 16, 128), F32),
            pltpu.VMEM((2, 7, 4, 16, 128), F32),
            pltpu.VMEM((4, 2, 16, 128), F32),
            pltpu.VMEM((3, 2, 16, 128), F32),
            pltpu.VMEM((2, 2, 8, 128), F32),
            pltpu.VMEM((2, 8, 128), F32),
            pltpu.VMEM((3, 8, 128), F32),
            pltpu.VMEM((3, 7, 8, 128), F32),
            pltpu.VMEM((256, 512), F32),
            dma, dma, dma((2, 8)), dma((2, 8)), dma((7,)), dma((7,)), dma((2, 4)), dma((2, 4)),
            dma((2, 8)), dma((2, 8)), dma((2, 8)), dma((2, 8)), dma((4,)), dma((4,)),
            dma((2, 2, 2, 4)), dma((2, 2, 2, 4)), dma((2, 7)), dma((2, 7)), dma((3,)), dma((3,)),
            dma, dma, dma((3, 7)), dma((3, 7)),
        ],
        compiler_params=pltpu.CompilerParams(
            collective_id=0, has_side_effects=True, vmem_limit_bytes=50 * 2**20
        ),
        cost_estimate=pl.CostEstimate(flops=3_221_225_472, bytes_accessed=5_000_000, transcendentals=0),
    )(normed_input, key_weight, key_cotangent)


def solution(mesh):
    placed = P(("node", "local"), None)
    return jax.shard_map(
        body, mesh=mesh, in_specs=(placed,) * 3, out_specs=(placed,) * 3, check_vma=False
    )
```

time: 953 us -> 69.2 us (0.07)
  waiting for transfers between devices: 704 us -> 0 us
  blocking collectives: 211 us -> 0 us
  Pallas kernels: 0 us -> 64 us
  between operations: 16.2 us -> 0.65 us
  matrix products: 11.2 us -> 0 us
    all_gather x2 -> x0, waiting for transfers between devices: 703 us -> none  [the longest x1 703 us: body(): lax.all_gather(key_weight, ('node', 'local'), axis=0, tiled=True)]
    psum x1 -> x0, blocking collectives: 106 us -> none  [body(): square_sum = lax.psum(jnp.sum(weight_grad * weight_grad), ('node', 'local'))]
    all_to_all x1 -> x0, blocking collectives: 105 us -> none  [body(): lax.all_to_all(term_blocks, 'local', split_axis=1, concat_axis=1, tiled=T...]
    pallas_call x0 -> x1, Pallas kernels: none -> 64 us  [body(): pl.pallas_call(kernel, out_shape=(jax.ShapeDtypeStruct((256, 512), BF16),...]
    dot_general x3 -> x0, matrix products: 11.2 us -> none  [the longest x1 4.8 us: body(): jnp.einsum('tc,nkc->tnk', key_cotangent, lax.all_gather(secondary, 'local...]
  transfers between devices with their start and end apart: 3 -> 0, of which waited for: 1 -> 0; matrix products, arithmetic and copies ran while one was open for 1% -> 0% of each run, Pallas kernels for 0% -> 0%
where the time goes in v1:
time: 69.2 us; the launch traced here: 68.9 us
  Pallas kernels  64 us (92%)
  local copies, waits for them, and re-layouts  4.27 us (6%)
    pallas_call x1, Pallas kernels, body(): pl.pallas_call(kernel, out_shape=(jax.ShapeDtypeStruct((256, 512), BF16),...  64 us
    unnamed x7, local copies, waits for them, and re-layouts  4.27 us

profile of v1, /device:TPU:1, one launch (start us, length us, event | category | flops | bytes accessed | tf_op | source)
XLA Modules:
  0.0 68.9 jit_solution(12669208832680428302)
XLA Ops:
  0.6 0.0 copy-start
  0.6 0.9 %copy-done = bf16[256,512]{1,0:T(8,128)(2,1)S(1)} copy-done((bf16[256,512]{1,0:T(8,128)(2,1)S(1)}, bf16[256,512]{1,0:T(8,128)(2,1)}, u32[]{:S(2)}) %copy-start) | copy-done | bytes 262168
  1.6 0.0 copy-start.1
  1.6 0.7 %copy-done.1 = bf16[8,512]{1,0:T(8,128)(2,1)S(1)} copy-done((bf16[8,512]{1,0:T(8,128)(2,1)S(1)}, bf16[8,512]{1,0:T(8,128)(2,1)}, u32[]{:S(2)}) %copy-start.1) | copy-done | bytes 8216
  2.3 64.0 %shard_map.58 = (bf16[256,512]{1,0:T(8,128)(2,1)S(1)}, bf16[256,4096]{1,0:T(8,128)(2,1)S(1)}, f32[8,512]{1,0:T(8,128)S(1)}) custom-call(bf16[256,4096]{1,0:T(8,128)(2,1)} %x_ref.1, bf16[8,512]{1,0:T(8,128)(2,1)S(1)} %copy-done.1, bf16[256,512]{1,0:T(8,128)(2,1)S(1)} %copy-done), custom_call_target="tpu_custom_call" | custom-call | flops 3221225472 | bytes 5000000 | tf_op jit(solution)/shard_map/pallas_call | solution.py:325
  66.3 0.7 %copy.9 = bf16[256,512]{1,0:T(8,128)(2,1)} copy(bf16[256,512]{1,0:T(8,128)(2,1)S(1)} %get-tuple-element.6) | data formatting | bytes 524288
  67.0 1.3 %copy.10 = bf16[256,4096]{1,0:T(8,128)(2,1)} copy(bf16[256,4096]{1,0:T(8,128)(2,1)S(1)} %get-tuple-element.7) | data formatting | bytes 4194304
  68.3 0.6 copy.11
Async XLA Ops:
  0.6 1.0 %copy-start = (bf16[256,512]{1,0:T(8,128)(2,1)S(1)}, bf16[256,512]{1,0:T(8,128)(2,1)}, u32[]{:S(2)}) copy-start(bf16[256,512]{1,0:T(8,128)(2,1)} %c_ref.1) | copy-start | bytes 786436
  1.6 0.7 %copy-start.1 = (bf16[8,512]{1,0:T(8,128)(2,1)S(1)}, bf16[8,512]{1,0:T(8,128)(2,1)}, u32[]{:S(2)}) copy-start(bf16[8,512]{1,0:T(8,128)(2,1)} %w_ref.1) | copy-start | bytes 24580

commit v2 on v1

--- a/solution.py
+++ b/solution.py
@@ -31,8 +31,8 @@
 
 
 def kernel(
-    x_ref, w_ref, c_ref, keys_ref, grad_ref, update_ref,
-    weight, shard, shard_in, away, pair_in, term, ring_in, block, block_in,
+    x_hbm, w_hbm, c_hbm, keys_ref, grad_ref, update_ref,
+    x_ref, w_ref, c_ref, in_s, weight, shard, shard_in, away, pair_in, term, ring_in, block, block_in,
     slab, slab_in, mine, mine_in, squares, squares_in, keys_sum,
     shard_s, shard_r, pair_s, pair_r, gz_s, gz_r, gy_s, gy_r, gx_s, gx_r, gf_s, gf_r, gc_s, gc_r,
     ring_s, ring_r, block_s, block_r, slab_s, slab_r, mine_s, mine_r, sq_s, sq_r,
@@ -64,7 +64,17 @@
     for device in greeted:
         pl.semaphore_signal(barrier, inc=1, device_id=device, device_id_type=MESH)
 
-    def terms_of(half, ref):
+    loads = [
+        pltpu.make_async_copy(c_hbm, c_ref, in_s.at[0]),
+        pltpu.make_async_copy(w_hbm, w_ref, in_s.at[1]),
+    ]
+    for i in range(4):
+        at = pl.ds(i * 1024, 1024)
+        loads.append(pltpu.make_async_copy(x_hbm.at[:, at], x_ref.at[:, at], in_s.at[2 + i]))
+    for load in loads:
+        load.start()
+
+    def terms_of(half, ref, lo, hi):
         cot = c_ref[:, pl.ds(pl.multiple_of(half * 256, 256), 256)]
 
         def one(zb, carry):
@@ -72,19 +82,23 @@
             t = lax.dot_general(
                 rows, cot, (((0,), (0,)), ((), ())), preferred_element_type=F32
             ).astype(BF16)
-            ref[0, zb] = t[:, :128].reshape(2, 4, 64, 128)
+            ref[0, zb] = t[:, :128].reshape(4, 2, 64, 128)
             tb = t[:, 128:].reshape(2, 4, 4, 16, 128)
             for yh in range(2):
                 for yl in range(4):
-                    ref[1, yh * 4 + yl, lax.div(zb, 4), lax.rem(zb, 4)] = tb[yh, :, yl].reshape(64, 128)
+                    ref[1, yh * 4 + yl, lax.div(zb, 2), lax.rem(zb, 2)] = tb[yh, :, yl].reshape(64, 128)
             return carry
 
-        lax.fori_loop(0, 8, one, 0)
-
+        lax.fori_loop(lo, hi, one, 0)
+
+    loads[0].wait()
+    loads[1].wait()
     w = w_ref[...].astype(F32)
     shard[0] = w[:, :256]
     shard[1] = w[:, 256:]
-    terms_of(sib, away)
+    for i in range(4):
+        loads[2 + i].wait()
+        terms_of(sib, away, 2 * i, 2 * i + 2)
     pl.semaphore_wait(barrier, len(greeted))
 
     start(copy_to(shard.at[sib], shard_in, shard_s, shard_r, sibling))
@@ -94,7 +108,6 @@
             b = mod(place[q] + o, 8)
             pairs[q, o] = copy_to(away.at[q, b], pair_in.at[q, b], pair_s.at[q, o], pair_r.at[q, o], sibling)
             start(pairs[q, o])
-    terms_of(c, term)
 
     yh, yl = lax.div(y, 4), lax.rem(y, 4)
     copy_to(shard.at[sib], shard_in, shard_s, shard_r, sibling).wait_recv()
@@ -106,41 +119,53 @@
         spot = weight.at[c, z, yh, x, yl]
         start(copy_to(spot, spot, gz_s.at[k - 1], gz_r.at[k - 1], along_z(k)))
 
-    def length(sign, u):
-        return 4 if (sign == 0) == (u == 0) else 3
-
-    waited = set()
-
-    def paired(q, o, u):
-        if (q, o % 8) not in waited:
-            waited.add((q, o % 8))
-            pairs[q, o % 8].wait_recv()
-        b = mod(place[q] + o, 8)
-        return b, term[q, b, u].astype(F32) + pair_in[q, b, u].astype(F32)
-
-    def ring_copy(q, sign, u, s, b):
+    terms_of(c, term, 0, 8)
+
+    def part_of(sign, v):
+        return v if sign == 0 else lax.rem(v + 2, 4)
+
+    def ring_copy(q, sign, v, s, b):
         return copy_to(
-            term.at[q, b, u],
-            ring_in.at[q, sign, u, s - 1],
-            ring_s.at[q, sign, u, s - 1],
-            ring_r.at[q, sign, u, s - 1],
+            term.at[q, b, part_of(sign, v)],
+            ring_in.at[q, sign, v, s - 1],
+            ring_s.at[q, sign, v, s - 1],
+            ring_r.at[q, sign, v, s - 1],
             along[q](1 - 2 * sign),
         )
 
-    def ring_step(s):
-        for u in range(2):
+    def pair_wait(*offsets):
+        for o in offsets:
+            for q in range(2):
+                pairs[q, o].wait_recv()
+
+    def ring_step(s, far):
+        n = 4 if far else 3
+
+        def one(i, carry):
+            v = i if far else i + 2
             for q in range(2):
                 for sign in range(2):
-                    n = length(sign, u)
-                    if s > n:
-                        continue
-                    o = (1 - 2 * sign) * (n - s + 1)
-                    b, total = paired(q, o, u)
+                    b = mod(place[q] + (1 - 2 * sign) * (n - s + 1), 8)
+                    u = part_of(sign, v)
+                    total = term[q, b, u].astype(F32) + pair_in[q, b, u].astype(F32)
                     if s > 1:
-                        ring_copy(q, sign, u, s - 1, b).wait_recv()
-                        total = total + ring_in[q, sign, u, s - 2].astype(F32)
+                        ring_copy(q, sign, v, s - 1, b).wait_recv()
+                        total = total + ring_in[q, sign, v, s - 2].astype(F32)
                     term[q, b, u] = total.astype(BF16)
-                    start(ring_copy(q, sign, u, s, b))
+                    ring_copy(q, sign, v, s, b).start()
+            return carry
+
+        lax.fori_loop(0, 2, one, 0)
+
+    def ring_sent():
+        for s in range(1, 5):
+            def one(v, carry):
+                for q in range(2):
+                    for sign in range(2):
+                        ring_copy(q, sign, v, s, 0).wait_send()
+                return carry
+
+            lax.fori_loop(0, 4 if s < 4 else 2, one, 0)
 
     def column(h, xo, yo, lo=0, n=8):
         yy = mod(y + yo, 8)
@@ -165,40 +190,64 @@
             col = column(c, 0, -(1 - 2 * sign) * s, lo, n)
             copy_to(col, col, gy_s.at[sign, s - 1], gy_r.at[sign, s - 1], along_y(1 - 2 * sign)).wait_recv()
 
-    ring_step(1)
+    def to_sibling(i, xo):
+        part = weight.at[c, :, :, mod(x + xo, NX)]
+        start(copy_to(part, part, gc_s.at[i], gc_r.at[i], sibling))
+
+    def forward_x(j):
+        for sign in range(2):
+            col = column(c, -(1 - 2 * sign), columns[j])
+            copy_to(col, col, gx_s.at[sign, j], gx_r.at[sign, j], along_x(1 - 2 * sign)).wait_recv()
+            half = column(c, -(1 - 2 * sign), columns[j], 4 * sign, 4)
+            start(copy_to(half, half, gf_s.at[sign, j], gf_r.at[sign, j], along_x(1 - 2 * sign)))
+
+    pair_wait(4)
+    ring_step(1, True)
+    pair_wait(3, 5)
+    ring_step(1, False)
     for k in range(1, NZ):
         spot = weight.at[c, mod(z - k, NZ), yh, x, yl]
         copy_to(spot, spot, gz_s.at[k - 1], gz_r.at[k - 1], along_z(k)).wait_recv()
     gather_y(1)
     send_x(0)
-    ring_step(2)
+    ring_step(2, True)
+    pair_wait(2, 6)
+    ring_step(2, False)
     gathered_y(1)
     gather_y(2)
     send_x(1)
     send_x(2)
-    ring_step(3)
+    ring_step(3, True)
+    pair_wait(1, 7)
+    ring_step(3, False)
     gathered_y(2)
     gather_y(3)
     send_x(3)
     send_x(4)
-    ring_step(4)
+    forward_x(0)
+    ring_step(4, True)
     gathered_y(3)
     gather_y(4)
     send_x(5)
     send_x(6)
-
-    for q in range(2):
-        for u in range(2):
-            b, total = paired(q, 0, u)
+    forward_x(1)
+    forward_x(2)
+
+    pair_wait(0)
+    for v in range(4):
+        for q in range(2):
+            total = term[q, place[q], v].astype(F32) + pair_in[q, place[q], v].astype(F32)
             for sign in range(2):
-                n = length(sign, u)
-                ring_copy(q, sign, u, n, b).wait_recv()
-                total = total + ring_in[q, sign, u, n - 1].astype(F32)
-            for j in range(4):
-                if q == 0:
-                    block[q, u * 4 + j] = total.reshape(4, 4, 16, 128)[:, j]
-                else:
-                    block[q, u * 4 + j] = total[j].reshape(4, 16, 128)
+                w_ = v if sign == 0 else (v + 2) % 4
+                n = 4 if w_ < 2 else 3
+                ring_copy(q, sign, w_, n, 0).wait_recv()
+                total = total + ring_in[q, sign, w_, n - 1].astype(F32)
+            if q == 0:
+                for yl in range(4):
+                    block[0, (v // 2) * 4 + yl, (v % 2) * 2 : (v % 2) * 2 + 2] = total.reshape(2, 4, 16, 128)[:, yl]
+            else:
+                block[1, 2 * v : 2 * v + 2] = total.reshape(2, 4, 16, 128)
+
     def block_copy(q, k):
         return copy_to(
             block.at[q, mod(across_place[q] + k, 8)], block_in.at[q, k - 1],
@@ -211,20 +260,9 @@
 
     gathered_y(4)
     send_x(7)
-
-    def to_sibling(i, xo):
-        part = weight.at[c, :, :, mod(x + xo, NX)]
-        start(copy_to(part, part, gc_s.at[i], gc_r.at[i], sibling))
-
     to_sibling(0, 0)
-    for j in range(8):
-        for sign in range(2):
-            col = column(c, -(1 - 2 * sign), columns[j])
-            copy_to(col, col, gx_s.at[sign, j], gx_r.at[sign, j], along_x(1 - 2 * sign)).wait_recv()
-            half = column(c, -(1 - 2 * sign), columns[j], 4 * sign, 4)
-            start(copy_to(half, half, gf_s.at[sign, j], gf_r.at[sign, j], along_x(1 - 2 * sign)))
-    to_sibling(1, -1)
-    to_sibling(2, 1)
+    forward_x(3)
+    forward_x(4)
 
     for q in range(2):
         total = block[q, across_place[q]]
@@ -238,12 +276,10 @@
 
     for k in range(1, NX):
         start(slab_copy(k))
-
-    for j in range(8):
-        for sign in range(2):
-            half = column(c, 2, columns[j], 4 * sign, 4)
-            copy_to(half, half, gf_s.at[sign, j], gf_r.at[sign, j], along_x(1 - 2 * sign)).wait_recv()
-    to_sibling(3, 2)
+    for j in range(5, 8):
+        forward_x(j)
+    to_sibling(1, -1)
+    to_sibling(2, 1)
 
     total = slab[x]
     for k in range(1, NX):
@@ -292,21 +328,37 @@
     def square_copy(i, k):
         return copy_to(squares.at[i], squares_in.at[i, k], sq_s.at[i, k], sq_r.at[i, k], groups[i][k])
 
-    parts = ((0, 3), (3, 6), (6, 8))
-    for i in range(3):
+    def square_send(i):
         squares[i] = sq
         for k in range(7):
             start(square_copy(i, k))
-        if i == 0:
-            for n, xo in enumerate((0, -1, 1, 2)):
-                part = weight.at[sib, :, :, mod(x + xo, NX)]
-                copy_to(part, part, gc_s.at[n], gc_r.at[n], sibling).wait_recv()
-        multiply(*parts[i])
-        if i == 2:
-            keys_ref[...] = keys_sum[...].astype(BF16)
+
+    def square_sum(i, sq):
         for k in range(7):
             square_copy(i, k).wait_recv()
             sq = sq + squares_in[i, k]
+        return sq
+
+    square_send(0)
+    for j in range(8):
+        for sign in range(2):
+            half = column(c, 2, columns[j], 4 * sign, 4)
+            copy_to(half, half, gf_s.at[sign, j], gf_r.at[sign, j], along_x(1 - 2 * sign)).wait_recv()
+    to_sibling(3, 2)
+    sq = square_sum(0, sq)
+    square_send(1)
+    for n, xo in enumerate((0, -1, 1, 2)):
+        part = weight.at[sib, :, :, mod(x + xo, NX)]
+        copy_to(part, part, gc_s.at[n], gc_r.at[n], sibling).wait_recv()
+    multiply(0, 5)
+    sq = square_sum(1, sq)
+    square_send(2)
+    multiply(5, 8)
+    keys_ref[...] = keys_sum[...].astype(BF16)
+    ring_sent()
+    for copy in sent[:-7]:
+        copy.wait_send()
+    sq = square_sum(2, sq)
 
     scale = lax.rsqrt(jnp.full((8, 128), jnp.sum(sq) / 2097152.0 + 1e-06, F32))
     copy_to(mine.at[sib], mine_in, mine_s, mine_r, sibling).wait_recv()
@@ -315,7 +367,7 @@
     for q in range(2):
         update_ref[:, q * 128 : q * 128 + 128] = jnp.where(c == 0, got[q], came[q]) * scale
         update_ref[:, 256 + q * 128 : 384 + q * 128] = jnp.where(c == 0, came[q], got[q]) * scale
-    for copy in sent:
+    for copy in sent[-7:]:
         copy.wait_send()
 
 
@@ -329,16 +381,20 @@
             jax.ShapeDtypeStruct((256, 4096), BF16),
             jax.ShapeDtypeStruct((8, 512), F32),
         ),
-        in_specs=[vmem] * 3,
+        in_specs=[pl.BlockSpec(memory_space=pltpu.HBM)] * 3,
         out_specs=(vmem,) * 3,
         scratch_shapes=[
+            pltpu.VMEM((256, 4096), BF16),
+            pltpu.VMEM((8, 512), BF16),
+            pltpu.VMEM((256, 512), BF16),
+            dma((6,)),
             pltpu.VMEM((2, NZ, 2, NX, 4, 16, 256), BF16),
             pltpu.VMEM((2, 8, 256), F32),
             pltpu.VMEM((8, 256), F32),
-            pltpu.VMEM((2, 8, 2, 4, 64, 128), BF16),
-            pltpu.VMEM((2, 8, 2, 4, 64, 128), BF16),
-            pltpu.VMEM((2, 8, 2, 4, 64, 128), BF16),
-            pltpu.VMEM((2, 2, 2, 4, 4, 64, 128), BF16),
+            pltpu.VMEM((2, 8, 4, 2, 64, 128), BF16),
+            pltpu.VMEM((2, 8, 4, 2, 64, 128), BF16),
+            pltpu.VMEM((2, 8, 4, 2, 64, 128), BF16),
+            pltpu.VMEM((2, 2, 4, 4, 2, 64, 128), BF16),
             pltpu.VMEM((2, 8, 4, 16, 128), F32),
             pltpu.VMEM((2, 7, 4, 16, 128), F32),
             pltpu.VMEM((4, 2, 16, 128), F32),
@@ -350,7 +406,7 @@
             pltpu.VMEM((256, 512), F32),
             dma, dma, dma((2, 8)), dma((2, 8)), dma((7,)), dma((7,)), dma((2, 4)), dma((2, 4)),
             dma((2, 8)), dma((2, 8)), dma((2, 8)), dma((2, 8)), dma((4,)), dma((4,)),
-            dma((2, 2, 2, 4)), dma((2, 2, 2, 4)), dma((2, 7)), dma((2, 7)), dma((3,)), dma((3,)),
+            dma((2, 2, 4, 4)), dma((2, 2, 4, 4)), dma((2, 7)), dma((2, 7)), dma((3,)), dma((3,)),
             dma, dma, dma((3, 7)), dma((3, 7)),
         ],
         compiler_params=pltpu.CompilerParams(

time: 69.2 us -> 66.2 us (0.957)
  Pallas kernels: 64 us -> 61.1 us
    pallas_call x1, Pallas kernels: 64 us -> 61.1 us  [body(): pl.pallas_call(kernel, out_shape=(jax.ShapeDtypeStruct((256, 512), BF16),...]
where the time goes in v2:
time: 66.2 us; the launch traced here: 66 us
  Pallas kernels  61.1 us (92%)
  local copies, waits for them, and re-layouts  4.27 us (6%)
    pallas_call x1, Pallas kernels, body(): pl.pallas_call(kernel, out_shape=(jax.ShapeDtypeStruct((256, 512), BF16),...  61.1 us
    unnamed x7, local copies, waits for them, and re-layouts  4.27 us

profile of v2, /device:TPU:1, one launch (start us, length us, event | category | flops | bytes accessed | tf_op | source)
XLA Modules:
  0.0 66.0 jit_solution(12447163693550780509)
XLA Ops:
  0.6 0.0 copy-start
  0.6 0.9 %copy-done = bf16[256,512]{1,0:T(8,128)(2,1)S(1)} copy-done((bf16[256,512]{1,0:T(8,128)(2,1)S(1)}, bf16[256,512]{1,0:T(8,128)(2,1)}, u32[]{:S(2)}) %copy-start) | copy-done | bytes 262168
  1.6 0.0 copy-start.1
  1.6 0.7 %copy-done.1 = bf16[8,512]{1,0:T(8,128)(2,1)S(1)} copy-done((bf16[8,512]{1,0:T(8,128)(2,1)S(1)}, bf16[8,512]{1,0:T(8,128)(2,1)}, u32[]{:S(2)}) %copy-start.1) | copy-done | bytes 8216
  2.3 61.1 %shard_map.58 = (bf16[256,512]{1,0:T(8,128)(2,1)S(1)}, bf16[256,4096]{1,0:T(8,128)(2,1)S(1)}, f32[8,512]{1,0:T(8,128)S(1)}) custom-call(bf16[256,4096]{1,0:T(8,128)(2,1)} %x_hbm.1, bf16[8,512]{1,0:T(8,128)(2,1)S(1)} %copy-done.1, bf16[256,512]{1,0:T(8,128)(2,1)S(1)} %copy-done), custom_call_target="tpu_custom_call" | custom-call | flops 3221225472 | bytes 5000000 | tf_op jit(solution)/shard_map/pallas_call | solution.py:377
  63.4 0.7 %copy.9 = bf16[256,512]{1,0:T(8,128)(2,1)} copy(bf16[256,512]{1,0:T(8,128)(2,1)S(1)} %get-tuple-element.6) | data formatting | bytes 524288
  64.1 1.3 %copy.10 = bf16[256,4096]{1,0:T(8,128)(2,1)} copy(bf16[256,4096]{1,0:T(8,128)(2,1)S(1)} %get-tuple-element.7) | data formatting | bytes 4194304
  65.4 0.6 copy.11
Async XLA Ops:
  0.6 1.0 %copy-start = (bf16[256,512]{1,0:T(8,128)(2,1)S(1)}, bf16[256,512]{1,0:T(8,128)(2,1)}, u32[]{:S(2)}) copy-start(bf16[256,512]{1,0:T(8,128)(2,1)} %c_hbm.1) | copy-start | bytes 786436
  1.6 0.7 %copy-start.1 = (bf16[8,512]{1,0:T(8,128)(2,1)S(1)}, bf16[8,512]{1,0:T(8,128)(2,1)}, u32[]{:S(2)}) copy-start(bf16[8,512]{1,0:T(8,128)(2,1)} %w_hbm.1) | copy-start | bytes 24580

commit v3 on v2

--- a/solution.py
+++ b/solution.py
@@ -110,6 +110,7 @@
             start(pairs[q, o])
 
     yh, yl = lax.div(y, 4), lax.rem(y, 4)
+    terms_of(c, term, 0, 4)
     copy_to(shard.at[sib], shard_in, shard_s, shard_r, sibling).wait_recv()
     own, other = shard[c], shard_in[...]
     first = jnp.where(c == 0, own, other)
@@ -119,7 +120,7 @@
         spot = weight.at[c, z, yh, x, yl]
         start(copy_to(spot, spot, gz_s.at[k - 1], gz_r.at[k - 1], along_z(k)))
 
-    terms_of(c, term, 0, 8)
+    terms_of(c, term, 4, 8)
 
     def part_of(sign, v):
         return v if sign == 0 else lax.rem(v + 2, 4)
@@ -344,12 +345,16 @@
         for sign in range(2):
             half = column(c, 2, columns[j], 4 * sign, 4)
             copy_to(half, half, gf_s.at[sign, j], gf_r.at[sign, j], along_x(1 - 2 * sign)).wait_recv()
-    to_sibling(3, 2)
+        col = column(c, 2, columns[j])
+        start(copy_to(col, col, gc_s.at[3 + j], gc_r.at[3 + j], sibling))
     sq = square_sum(0, sq)
     square_send(1)
-    for n, xo in enumerate((0, -1, 1, 2)):
+    for n, xo in enumerate((0, -1, 1)):
         part = weight.at[sib, :, :, mod(x + xo, NX)]
         copy_to(part, part, gc_s.at[n], gc_r.at[n], sibling).wait_recv()
+    for j in range(8):
+        col = column(sib, 2, columns[j])
+        copy_to(col, col, gc_s.at[3 + j], gc_r.at[3 + j], sibling).wait_recv()
     multiply(0, 5)
     sq = square_sum(1, sq)
     square_send(2)
@@ -405,7 +410,7 @@
             pltpu.VMEM((3, 7, 8, 128), F32),
             pltpu.VMEM((256, 512), F32),
             dma, dma, dma((2, 8)), dma((2, 8)), dma((7,)), dma((7,)), dma((2, 4)), dma((2, 4)),
-            dma((2, 8)), dma((2, 8)), dma((2, 8)), dma((2, 8)), dma((4,)), dma((4,)),
+            dma((2, 8)), dma((2, 8)), dma((2, 8)), dma((2, 8)), dma((11,)), dma((11,)),
             dma((2, 2, 4, 4)), dma((2, 2, 4, 4)), dma((2, 7)), dma((2, 7)), dma((3,)), dma((3,)),
             dma, dma, dma((3, 7)), dma((3, 7)),
         ],

time: 66.2 us -> 67.2 us (1.015)
  Pallas kernels: 61.1 us -> 62 us
    pallas_call x1, Pallas kernels: 61.1 us -> 62 us  [body(): pl.pallas_call(kernel, out_shape=(jax.ShapeDtypeStruct((256, 512), BF16),...]
where the time goes in v3:
time: 67.2 us; the launch traced here: 66.9 us
  Pallas kernels  62 us (92%)
  local copies, waits for them, and re-layouts  4.27 us (6%)
    pallas_call x1, Pallas kernels, body(): pl.pallas_call(kernel, out_shape=(jax.ShapeDtypeStruct((256, 512), BF16),...  62 us
    unnamed x7, local copies, waits for them, and re-layouts  4.27 us

profile of v3, /device:TPU:1, one launch (start us, length us, event | category | flops | bytes accessed | tf_op | source)
XLA Modules:
  0.0 66.9 jit_solution(14352880852093368220)
XLA Ops:
  0.6 0.0 copy-start
  0.6 0.9 %copy-done = bf16[256,512]{1,0:T(8,128)(2,1)S(1)} copy-done((bf16[256,512]{1,0:T(8,128)(2,1)S(1)}, bf16[256,512]{1,0:T(8,128)(2,1)}, u32[]{:S(2)}) %copy-start) | copy-done | bytes 262168
  1.6 0.0 copy-start.1
  1.6 0.7 %copy-done.1 = bf16[8,512]{1,0:T(8,128)(2,1)S(1)} copy-done((bf16[8,512]{1,0:T(8,128)(2,1)S(1)}, bf16[8,512]{1,0:T(8,128)(2,1)}, u32[]{:S(2)}) %copy-start.1) | copy-done | bytes 8216
  2.3 62.0 %shard_map.58 = (bf16[256,512]{1,0:T(8,128)(2,1)S(1)}, bf16[256,4096]{1,0:T(8,128)(2,1)S(1)}, f32[8,512]{1,0:T(8,128)S(1)}) custom-call(bf16[256,4096]{1,0:T(8,128)(2,1)} %x_hbm.1, bf16[8,512]{1,0:T(8,128)(2,1)S(1)} %copy-done.1, bf16[256,512]{1,0:T(8,128)(2,1)S(1)} %copy-done), custom_call_target="tpu_custom_call" | custom-call | flops 3221225472 | bytes 5000000 | tf_op jit(solution)/shard_map/pallas_call | solution.py:382
  64.3 0.7 %copy.9 = bf16[256,512]{1,0:T(8,128)(2,1)} copy(bf16[256,512]{1,0:T(8,128)(2,1)S(1)} %get-tuple-element.6) | data formatting | bytes 524288
  65.0 1.3 %copy.10 = bf16[256,4096]{1,0:T(8,128)(2,1)} copy(bf16[256,4096]{1,0:T(8,128)(2,1)S(1)} %get-tuple-element.7) | data formatting | bytes 4194304
  66.3 0.6 copy.11
Async XLA Ops:
  0.6 1.0 %copy-start = (bf16[256,512]{1,0:T(8,128)(2,1)S(1)}, bf16[256,512]{1,0:T(8,128)(2,1)}, u32[]{:S(2)}) copy-start(bf16[256,512]{1,0:T(8,128)(2,1)} %c_hbm.1) | copy-start | bytes 786436
  1.6 0.7 %copy-start.1 = (bf16[8,512]{1,0:T(8,128)(2,1)S(1)}, bf16[8,512]{1,0:T(8,128)(2,1)}, u32[]{:S(2)}) copy-start(bf16[8,512]{1,0:T(8,128)(2,1)} %w_hbm.1) | copy-start | bytes 24580
